TPU v7x, 512 devices: a whole 4x8x8 slice. The times are simulated.
512 devices in a mesh: dp: 16 (over z, y_hi), seq: 8 (over y_lo, core), tensor: 4 (over x).
Axes of the slice: x: 4, y: 8 (y_hi: 2, y_lo: 4; y = y_hi * 4 + y_lo), z: 8, core: 2. Of those that a mesh axis runs over, the one named last changes fastest.
Arguments:
- activations: bfloat16 [32768, 512], P(('dp', 'seq')), may hold values from -6 to 6
- d_logits: bfloat16 [32768, 8192], P(('dp', 'seq'), 'tensor'), may hold values from -0.015625 to 0.015625
- block_owner: int32 [16], replicated, may hold values from 0 to 15, each once
- left_stat: float32 [16, 512, 512], P('dp', ('seq', 'tensor')), may hold values from -0.1 to 2.1
- right_stat: float32 [16, 512, 512], P('dp', ('seq', 'tensor')), may hold values from -0.1 to 2.1
- second_moment: float32 [16, 512, 512], P('dp', ('seq', 'tensor')), may hold values from 2e-05 to 0.002
- left_root: float32 [16, 512, 512], P('dp', ('seq', 'tensor')), may hold values from -0.15 to 14
- right_root: float32 [16, 512, 512], P('dp', ('seq', 'tensor')), may hold values from -0.15 to 14
Outputs:
- update: bfloat16 [16, 512, 512], P(None, ('seq', 'tensor'))
- left_new: float32 [16, 512, 512], P('dp', ('seq', 'tensor'))
- right_new: float32 [16, 512, 512], P('dp', ('seq', 'tensor'))
- moment_new: float32 [16, 512, 512], P('dp', ('seq', 'tensor'))
All inputs are finite; a program needn't handle non-finite values.
Results may differ from a plain program's by a relative error of at most 0.00055.
Values may be sent and summed in bfloat16 or wider, within the bound.
A program may use at most 64 MiB of HBM per device.

v0:
```python
import jax
import jax.numpy as jnp
from jax import lax
from jax.sharding import PartitionSpec as P

highest = lax.Precision.HIGHEST


def gradient_rows(logit_columns, activations):
    return lax.dot_general(
        logit_columns, activations, (((0,), (0,)), ((), ())), preferred_element_type=jnp.float32
    )


def per_device(
    activations, d_logits, block_owner, left_stat, right_stat, second_moment, left_root, right_root
):
    tokens_here = d_logits.shape[0]
    block_count = block_owner.shape[0]
    block_width = activations.shape[1]
    seq_count = lax.axis_size("seq")
    tensor_count = lax.axis_size("tensor")
    row_share = block_width // (seq_count * tensor_count)
    block_band = block_width // tensor_count
    indices = jnp.arange(block_count, dtype=jnp.int32)
    matches = block_owner[None, :] == indices[:, None]
    owner_block = jnp.sum(jnp.where(matches, indices[None, :], 0), axis=1)
    by_owner = jnp.take(d_logits.reshape(tokens_here, block_count, block_band), owner_block, axis=1)
    by_owner = by_owner.reshape(tokens_here, block_count * block_band)
    grad_slab = lax.psum_scatter(
        gradient_rows(by_owner, activations), ("dp", "seq"), scatter_dimension=0, tiled=True
    )
    moment_next = 0.99 * second_moment[0] + 0.01 * grad_slab * grad_slab
    adam_dir = grad_slab / (jnp.sqrt(moment_next) + 1e-08)
    adam_part = jnp.sum(adam_dir * adam_dir)
    adam_total = lax.psum(adam_part, ("seq", "tensor"))
    first_row = (lax.axis_index("seq") * tensor_count + lax.axis_index("tensor")) * row_share
    left_rows = left_root[0]
    slab_rows = lax.all_gather(grad_slab, ("seq", "tensor"), axis=0, tiled=True)
    outer_rows = jnp.dot(
        grad_slab, slab_rows.T, precision=highest, preferred_element_type=jnp.float32
    )
    own_columns = lax.dynamic_slice_in_dim(slab_rows, first_row, row_share, 1)
    right_part = jnp.dot(
        own_columns.T, slab_rows, precision=highest, preferred_element_type=jnp.float32
    )
    mixed_part = jnp.dot(
        left_rows, slab_rows, precision=highest, preferred_element_type=jnp.float32
    )
    left_next = 0.95 * left_stat[0] + outer_rows
    right_next = 0.95 * right_stat[0] + right_part
    precond = jnp.dot(
        mixed_part,
        lax.all_gather(right_root[0], ("seq", "tensor"), axis=0, tiled=True),
        precision=highest,
        preferred_element_type=jnp.float32,
    )
    precond_part = jnp.sum(precond * precond)
    precond_total = lax.psum(precond_part, ("seq", "tensor"))
    graft_scale = jnp.sqrt(adam_total) / (jnp.sqrt(precond_total) + 1e-06)
    update_rows = (graft_scale * precond).astype(jnp.bfloat16)
    gathered = lax.all_gather(update_rows[None], "dp", axis=0, tiled=True)
    update = jnp.take(gathered, block_owner, axis=0)
    return (update, left_next[None], right_next[None], moment_next[None])


def solution(mesh):
    return jax.shard_map(
        per_device,
        mesh=mesh,
        in_specs=(
            P(("dp", "seq"), None),
            P(("dp", "seq"), "tensor"),
            P(),
            P("dp", ("seq", "tensor"), None),
            P("dp", ("seq", "tensor"), None),
            P("dp", ("seq", "tensor"), None),
            P("dp", ("seq", "tensor"), None),
            P("dp", ("seq", "tensor"), None),
        ),
        out_specs=(
            P(None, ("seq", "tensor"), None),
            P("dp", ("seq", "tensor"), None),
            P("dp", ("seq", "tensor"), None),
            P("dp", ("seq", "tensor"), None),
        ),
        check_vma=False,
    )
```

profile of v0, /device:TPU:1, one launch (start us, length us, event | category | flops | bytes accessed | tf_op | source)
XLA Modules:
  0.0 526.9 jit_solution(10897611241762053604)
XLA Ops:
  7.2 0.0 copy-start
  7.2 0.0 reduce-scatter.2.cloned.1.call-start
  7.2 0.8 select_reduce_fusion
  8.1 1.5 copy.15
  9.6 0.7 copy.16
  10.2 0.7 gather_fusion
  11.0 0.5 copy.17
  11.5 0.1 broadcast_bitcast_fusion
  11.6 0.5 bitcast_select_fusion
  12.1 0.0 copy-done
  12.1 2.6 fusion.11
  14.8 0.0 copy-start.6
  14.8 0.0 copy-start.2
  14.8 0.0 copy-start.3
  14.8 0.0 copy-start.4
  14.8 0.0 copy-start.5
  14.8 0.0 reduce-scatter.2.cloned.1.call-update
  14.8 0.0 all-gather.5.cloned.1.call-start
  14.9 202.4 %reduce-scatter.2.cloned.1.call-done = f32[16,512]{1,0:T(8,128)} async-done(((f32[2048,512]{1,0:T(8,128)}), f32[16,512]{1,0:T(8,128)}) %reduce-scatter.2.cloned.1.call-update) | async-done | bytes 32784 | tf_op jit(solution)/shard_map/reduce_scatter | solution.py:30
  217.2 0.0 all-gather.5.cloned.1.call-update
  217.2 0.0 all-gather.7.cloned.1.call-start
  217.3 0.7 all-gather.7.cloned.1.call-update
  218.0 0.0 copy-done.6
  218.0 0.0 copy-done.2
  218.1 2.0 fusion.8
  220.0 88.5 %all-gather.5.cloned.1.call-done = f32[512,512]{1,0:T(8,128)} async-done(((f32[16,512]{1,0:T(8,128)}), f32[512,512]{1,0:T(8,128)}) %all-gather.5.cloned.1.call-update) | async-done | bytes 1048592 | tf_op jit(solution)/shard_map/all_gather | solution.py:39
  308.6 0.0 copy-done.3
  308.6 0.0 copy-start.1
  308.6 2.0 fusion.6
  310.5 87.3 %all-gather.7.cloned.1.call-done = f32[1,512,512]{2,1,0:T(8,128)} async-done(((f32[1,16,512]{2,1,0:T(8,128)}), f32[1,512,512]{2,1,0:T(8,128)}) %all-gather.7.cloned.1.call-update) | async-done | bytes 1048592 | tf_op jit(solution)/shard_map/all_gather | solution.py:54
  397.8 2.4 multiply_reduce_fusion
  400.3 67.3 %all-reduce = (f32[]{:T(128)}, f32[]{:T(128)}) all-reduce(f32[]{:T(128)} %get-tuple-element.7, f32[]{:T(128)} %get-tuple-element.8), channel_id=1, replica_groups=mesh['dp'=16,'seq'=8,'tensor'=4] {'seq','tensor'}, use_global_device_ids=true, to_apply=%region_3.4 | all-reduce | flops 2 | bytes 16 | tf_op jit(solution)/shard_map/psum | solution.py:36
  469.0 46.3 %all-gather.1 = bf16[256,512]{1,0:T(8,128)(2,1)S(1)} all-gather(bf16[16,512]{1,0:T(8,128)(2,1)S(1)} %multiply_convert_fusion), channel_id=3, replica_groups=mesh['dp'=16,'seq'=8,'tensor'=4] {'dp'}, dimensions={0}, use_global_device_ids=true | all-gather | bytes 278528 | tf_op jit(solution)/shard_map/all_gather | solution.py:62
  515.3 0.6 gather_fusion.1
  515.9 0.8 broadcast_select_fusion
  516.7 0.0 copy-done.4
  516.7 0.0 copy-done.1
  516.7 2.3 fusion
  519.1 0.0 copy-done.5
  519.1 1.3 fusion.1
  (7 shorter events, 0.0 us)
Async XLA Ops:
  7.2 5.0 copy-start
  7.2 210.0 %reduce-scatter.2.cloned.1.call-start = ((), (), s32[]{:S(2)}) async-start(), calls=%async_computation.1 | async-start | bytes 4227072 | tf_op jit(solution)/shard_map/reduce_scatter | solution.py:30
  14.8 203.2 %copy-start.6 = (s32[16]{0:T(128)S(1)}, s32[16]{0:T(128)}, u32[]{:S(2)}) copy-start(s32[16]{0:T(128)} %param.10) | copy-start | bytes 196
  14.8 203.3 %copy-start.2 = (f32[1,16,512]{2,1,0:T(8,128)S(1)}, f32[1,16,512]{2,1,0:T(8,128)}, u32[]{:S(2)}) copy-start(f32[1,16,512]{2,1,0:T(8,128)} %param.13) | copy-start | bytes 98308
  14.8 293.8 %copy-start.3 = (f32[1,16,512]{2,1,0:T(8,128)S(1)}, f32[1,16,512]{2,1,0:T(8,128)}, u32[]{:S(2)}) copy-start(f32[1,16,512]{2,1,0:T(8,128)} %param.14) | copy-start | bytes 98308
  14.8 501.9 %copy-start.4 = (f32[1,16,512]{2,1,0:T(8,128)S(1)}, f32[1,16,512]{2,1,0:T(8,128)}, u32[]{:S(2)}) copy-start(f32[1,16,512]{2,1,0:T(8,128)} %param.11) | copy-start | bytes 98308
  14.8 504.3 %copy-start.5 = (f32[1,16,512]{2,1,0:T(8,128)S(1)}, f32[1,16,512]{2,1,0:T(8,128)}, u32[]{:S(2)}) copy-start(f32[1,16,512]{2,1,0:T(8,128)} %param.12) | copy-start | bytes 98308
  14.8 293.7 %all-gather.5.cloned.1.call-start = ((), (), s32[]{:S(2)}) async-start(), calls=%async_computation.2 | async-start | bytes 1081344 | tf_op jit(solution)/shard_map/all_gather | solution.py:39
  217.2 180.6 %all-gather.7.cloned.1.call-start = ((), (), s32[]{:S(2)}) async-start(), calls=%async_computation.3 | async-start | bytes 1081344 | tf_op jit(solution)/shard_map/all_gather | solution.py:54
  308.6 208.1 %copy-start.1 = (f32[512,512]{1,0:T(8,128)S(1)}, f32[512,512]{1,0:T(8,128)}, u32[]{:S(2)}) copy-start(f32[512,512]{1,0:T(8,128)} %all-gather.5.cloned.1.call-done) | copy-start | bytes 3145732
Sparse Core Ops, SparseCore 0:
  14.9 202.2 reduce-scatter.1
  219.5 88.9 all-gather.4
  310.9 86.9 all-gather.6
where the time goes:
time: 537 us; the launch traced here: 527 us
  waiting for transfers between devices  379 us (71%)
  blocking collectives  114 us (21%)
  between operations  15.3 us (3%)
  matrix products  10.7 us (2%)
    reduce_scatter x1, waiting for transfers between devices, per_device(): lax.psum_scatter(gradient_rows(by_owner, activations), ('dp', 'seq'), sca...  202 us
    all_gather x1, waiting for transfers between devices, per_device(): slab_rows = lax.all_gather(grad_slab, ('seq', 'tensor'), axis=0, tiled=True)  88.5 us
    all_gather x1, waiting for transfers between devices, per_device(): lax.all_gather(right_root[0], ('seq', 'tensor'), axis=0, tiled=True)  87.3 us
    psum x1, blocking collectives, per_device(): adam_total = lax.psum(adam_part, ('seq', 'tensor'))  67.3 us
    all_gather x1, blocking collectives, per_device(): gathered = lax.all_gather(update_rows[None], 'dp', axis=0, tiled=True)  46.3 us
  transfers between devices with their start and end apart: 3, of which 3 were waited for; matrix products, arithmetic and copies ran while one was open for 1% of the time, Pallas kernels for 0%

commit v1 on v0

v1 whole, which is shorter than its diff:
```python
import jax
import jax.numpy as jnp
from jax import lax
from jax.experimental import pallas as pl
from jax.experimental.pallas import tpu as pltpu
from jax.sharding import PartitionSpec as P

F32 = jnp.float32
BF16 = jnp.bfloat16
MESH = pl.DeviceIdType.MESH

NZ = 8
NY = 8
NL = 4
NX = 4
PIECES = 4
PIECE_ORDER = ((2, 3, 0, 1), (0, 1, 2, 3))


def split(value):
    high = value.astype(BF16)
    return high, (value - high.astype(F32)).astype(BF16)


def dot(a, b):
    return jnp.dot(a, b, preferred_element_type=F32)


def dot_nt(a, b):
    return lax.dot_general(a, b, (((1,), (1,)), ((), ())), preferred_element_type=F32)


def dot_tn(a, b):
    return lax.dot_general(a, b, (((0,), (0,)), ((), ())), preferred_element_type=F32)


def sum_all(value):
    return jnp.sum(jnp.sum(value, axis=0, keepdims=True), axis=1, keepdims=True)


def kernel(
    owner_ref, owned_ref, acts_ref, logit_ref, left_ref, right_ref, moment_ref, lroot_ref, rroot_ref,
    update_out, left_out, right_out, moment_out,
    logit_own, logit_other, acts_other, part, ring_in, axis_in, grad, rroot, grad_hi, grad_lo,
    rroot_hi, rroot_lo, columns, norms, updates,
    load_done, ex_send, ex_recv, ring_send, ring_recv, axis_send, axis_recv, gather_send, gather_recv,
    norm_send, norm_recv, update_send, update_recv,
):
    dp = lax.axis_index("dp")
    seq = lax.axis_index("seq")
    x = lax.axis_index("tensor")
    z, yh = dp // 2, dp % 2
    yl, c = seq // 2, seq % 2
    y = yh * NL + yl
    half = acts_ref.shape[1] // 2

    def at_yz(y_to, z_to):
        return (z_to * 2 + y_to // NL, (y_to % NL) * 2 + c, x)

    def in_group(yl_to, c_to, x_to):
        return (dp, yl_to * 2 + c_to, x_to)

    sibling = in_group(yl, 1 - c, x)
    i = (1 - c) * z + c * y
    me2 = (1 - c) * y + c * z

    def on_first(k):
        return at_yz((1 - c) * y + c * k, (1 - c) * k + c * z)

    def on_second(k):
        return at_yz((1 - c) * k + c * y, (1 - c) * z + c * k)

    ring_next = on_first((i + 1) % 8)
    ring_prev = on_first((i + 7) % 8)
    x_next, x_prev, x_far = (x + 1) % NX, (x + 3) % NX, (x + 2) % NX

    for b in range(owner_ref.shape[0]):
        band = logit_ref.shape[1] // owner_ref.shape[0]
        pltpu.make_async_copy(logit_ref.at[:, pl.ds(b * band, band)], logit_own.at[b], load_done).start()

    barrier = pltpu.get_barrier_semaphore()

    def signal(device):
        pl.semaphore_signal(barrier, inc=1, device_id=device, device_id_type=MESH)

    partners = 0
    for dx in range(NX):
        for dy in range(NL):
            for dc in range(2):
                if dx or dy or dc:
                    signal(in_group((yl + dy) % NL, (c + dc) % 2, (x + dx) % NX))
                    partners += 1
    for k in range(NL):
        signal(at_yz((1 - yh) * NL + k, z))
        partners += 1
    for k in range(1, NZ):
        signal(at_yz(y, (z + k) % NZ))
        partners += 1
    pl.semaphore_wait(barrier, partners)

    def remote(src, dst, send, recv, device):
        return pltpu.make_async_remote_copy(
            src_ref=src, dst_ref=dst, send_sem=send, recv_sem=recv,
            device_id=device, device_id_type=MESH,
        )

    blocks = owner_ref.shape[0]
    band = logit_ref.shape[1] // blocks
    exchange = [
        remote(
            acts_ref.at[:, pl.ds(pl.multiple_of((1 - c) * half, half), half)],
            acts_other, ex_send.at[0], ex_recv.at[0], sibling,
        )
    ]
    exchange[0].start()
    for b in range(blocks):
        strip = logit_ref.at[:, pl.ds(b * band, band)]
        remote(strip, logit_other.at[b], ex_send.at[1], ex_recv.at[1], sibling).start()
    exchange.append(remote(logit_other, logit_other, ex_send.at[1], ex_recv.at[1], sibling))

    def gather(which, slab):
        sent = []

        def arrive(q, core, column):
            place = slab(q, core, column)
            remote(
                place, place, gather_send.at[which, 0], gather_recv.at[which, core, q, column], sibling
            ).wait_recv()

        def push(q, column, device):
            place = slab(q, c, column)
            copy = remote(
                place, place, gather_send.at[which, len(sent)],
                gather_recv.at[which, c, q, column], device,
            )
            copy.start()
            sent.append(copy)

        to_next, to_prev = in_group(yl, c, x_next), in_group(yl, c, x_prev)

        def begin():
            push(yl, x, to_next)
            push(yl, x, to_prev)
            for dy in range(1, NL):
                push(yl, x, in_group((yl + dy) % NL, c, x))
            push(yl, x, sibling)

        def middle():
            arrive(yl, c, x_prev)
            push(yl, x_prev, to_next)
            push(yl, x_prev, sibling)
            arrive(yl, c, x_next)
            push(yl, x_next, sibling)
            for dy in range(1, NL):
                q = (yl + NL - dy) % NL
                arrive(q, c, x)
                push(q, x, to_next)
                push(q, x, to_prev)
                push(q, x, sibling)

        def late():
            for dy in range(1, NL):
                q = (yl + NL - dy) % NL
                arrive(q, c, x_prev)
                if dy == 1:
                    push(q, x_prev, to_next)
                push(q, x_prev, sibling)
                arrive(q, c, x_next)
                if dy >= 2:
                    push(q, x_next, to_prev)
                push(q, x_next, sibling)

        def end():
            for dy in range(NL):
                q = (yl + NL - dy) % NL
                arrive(q, c, x_far)
                push(q, x_far, sibling)
            for dx in range(NX):
                for dy in range(NL):
                    arrive((yl + dy) % NL, 1 - c, (x + dx) % NX)

        return begin, middle, late, end, sent

    rroot[yl, c, x] = rroot_ref[0]
    r_begin, r_middle, r_late, r_end, r_sent = gather(0, lambda q, core, column: rroot.at[q, core, column])
    g_begin, g_middle, g_late, g_end, g_sent = gather(1, lambda q, core, column: grad.at[core, q, :, column])
    r_begin()

    unit = band // NL

    def place(d, q):
        row = (d % 2) * NL + q
        return (1 - c) * ((d // 2) * 8 + row) + c * (row * 8 + d // 2)

    acts_own = acts_ref[:, pl.ds(pl.multiple_of(c * half, half), half)]

    def own_block(d, carry):
        rows = dot_tn(logit_own[owned_ref[d]], acts_own)
        for q in range(NL):
            part[place(d, q)] = rows[q * unit : (q + 1) * unit]
        return carry

    pltpu.make_async_copy(logit_own, logit_own, load_done).wait()
    lax.fori_loop(0, blocks, own_block, 0)
    r_middle()
    for copy in exchange:
        copy.wait_recv()

    acts_rest = acts_other[...]

    def other_block(d, carry):
        rows = dot_tn(logit_other[owned_ref[d]], acts_rest)
        for q in range(NL):
            spot = place(d, q)
            part[spot] = part[spot] + rows[q * unit : (q + 1) * unit]
        return carry

    lax.fori_loop(0, blocks, other_block, 0)

    def chunk(way, step):
        return (i + 4 - step) % 8 if way == 0 else (i + 4 + step) % 8

    def ring(way, step, piece):
        return remote(
            part.at[pl.ds(chunk(way, step) * 8 + 2 * piece, 2)],
            ring_in.at[way, step, pl.ds(2 * piece, 2)],
            ring_send.at[way, step, piece], ring_recv.at[way, step, piece],
            (ring_next, ring_prev)[way],
        )

    def first_pieces(way):
        return (0, 1) if way == 0 else (2, 3)

    def ring_add(spot, way, step, piece):
        ring(way, step, piece).wait_recv()
        rows = pl.ds(spot * 8 + 2 * piece, 2)
        part[rows] = part[rows] + ring_in[way, step, pl.ds(2 * piece, 2)]

    for k in range(2):
        for way in range(2):
            ring(way, 0, first_pieces(way)[k]).start()
    for k in range(2):
        for way in range(2):
            ring(way, 1, PIECE_ORDER[way][k]).start()
    r_late()
    for step in range(1, 4):
        for k in range(PIECES):
            for way in range(2):
                piece = PIECE_ORDER[way][k]
                if step == 1 and k < 2:
                    continue
                ring_add(chunk(way, step), way, step - 1, piece)
                ring(way, step, piece).start()

    def axis_copy(j):
        return remote(
            part.at[i * 8 + j], axis_in.at[me2], axis_send.at[j], axis_recv.at[me2], on_second(j)
        )

    for k in range(PIECES):
        for way in range(2):
            ring_add(i, way, 3, PIECE_ORDER[way][k])
        for piece in {2: (0, 2), 3: (1, 3)}.get(k, ()):
            for j in (2 * piece, 2 * piece + 1):

                @pl.when(j != me2)
                def _():
                    axis_copy(j).start()

    r_end()
    value = rroot[...].reshape(rroot_hi.shape)
    rroot_hi[...], rroot_lo[...] = split(value)

    total = part[i * 8 + me2]
    for k in range(1, 8):
        j = (me2 + k) % 8
        remote(part.at[i * 8 + j], axis_in.at[j], axis_send.at[j], axis_recv.at[j], sibling).wait_recv()
        total = total + axis_in[j]
    grad[c, yl, :, x] = total.reshape(2, unit // 2, half)

    g_begin()
    g_middle()
    g_late()
    g_end()

    own = jnp.concatenate([grad[0, yl, c, x], grad[1, yl, c, x]], axis=1)
    moment = 0.99 * moment_ref[0] + 0.01 * own * own
    moment_out[0] = moment
    adam = own / (jnp.sqrt(moment) + 1e-08)
    adam_part = sum_all(adam * adam)

    for s in range(2):
        grad_hi[s], grad_lo[s] = split(grad[s].reshape(grad_hi.shape[1:]))

    def times_grad(value):
        rows = value.shape[0]
        high, low = split(value)
        both = jnp.concatenate([high, low], axis=0)
        out = []
        for s in range(2):
            wide = dot(both, grad_hi[s])
            out.append(wide[:rows] + (wide[rows:] + dot(high, grad_lo[s])))
        return jnp.concatenate(out, axis=1)

    mixed = times_grad(lroot_ref[0])
    mixed_hi, mixed_lo = split(mixed)
    wide = dot(jnp.concatenate([mixed_hi, mixed_lo], axis=0), rroot_hi[...])
    count = mixed.shape[0]
    precond = wide[:count] + (wide[count:] + dot(mixed_hi, rroot_lo[...]))
    precond_part = sum_all(precond * precond)

    lanes = norms.shape[2]
    rank = (yl * 2 + c) * NX + x
    norms[rank] = jnp.concatenate(
        [jnp.broadcast_to(adam_part, (1, lanes)), jnp.broadcast_to(precond_part, (1, lanes))], axis=0
    )
    for dx in range(NX):
        for dy in range(NL):
            for dc in range(2):
                if dx or dy or dc:
                    remote(
                        norms.at[rank], norms.at[rank], norm_send, norm_recv,
                        in_group((yl + dy) % NL, (c + dc) % 2, (x + dx) % NX),
                    ).start()

    own_hi, own_lo = split(own)
    both = jnp.concatenate([own_hi, own_lo], axis=0)
    outer = 0.95 * left_ref[0]
    for s in range(2):
        span = slice(s * half, (s + 1) * half)
        wide = dot_nt(both[:, span], grad_hi[s])
        outer = outer + (wide[:count] + (wide[count:] + dot_nt(own_hi[:, span], grad_lo[s])))
    left_out[0] = outer

    everyone = norms.at[pl.ds(0, norms.shape[0] - 1)]
    remote(everyone, everyone, norm_send, norm_recv, sibling).wait()
    sums = jnp.sum(norms[...], axis=0)
    scale = jnp.sqrt(sums[0:1, 0:1]) / (jnp.sqrt(sums[1:2, 0:1]) + 1e-06)
    updates[dp] = (scale * precond).astype(BF16)

    def update_copy(d, k, device):
        return remote(updates.at[d], updates.at[d], update_send.at[k], update_recv.at[d], device)

    across = z * 2 + (1 - yh)
    update_sent = [update_copy(dp, 0, at_yz((1 - yh) * NL + yl, z))]
    for k in range(1, NZ):
        update_sent.append(update_copy(dp, k, at_yz(y, (z + k) % NZ)))
    for copy in update_sent:
        copy.start()
    update_copy(across, 0, sibling).wait_recv()
    for k in range(1, NZ):
        copy = update_copy(across, NZ - 1 + k, at_yz(y, (z + k) % NZ))
        copy.start()
        update_sent.append(copy)

    first = seq * (NX * count) + x * count
    lane = 128
    side = first // half
    tile = grad_hi.shape[1]
    strip = grad[side, :, :, :, :, pl.ds(pl.multiple_of((first % half) // lane * lane, lane), lane)]
    columns[...] = strip.reshape(tile, lane).T
    picked = columns[pl.ds(pl.multiple_of(first % lane, count), count)]
    right_out[0] = 0.95 * right_ref[0] + times_grad(picked)

    for k in range(1, NZ):
        for side_y in range(2):
            update_copy(((z + k) % NZ) * 2 + side_y, 0, sibling).wait_recv()
    for b in range(blocks):
        update_out[b] = updates[owner_ref[b]]

    for copy in exchange:
        copy.wait_send()
    for way in range(2):
        for piece in first_pieces(way):
            ring(way, 0, piece).wait_send()
        for step in range(1, 4):
            for piece in range(PIECES):
                ring(way, step, piece).wait_send()
    for k in range(1, 8):
        axis_copy((me2 + k) % 8).wait_send()
    for copy in r_sent + g_sent + update_sent:
        copy.wait_send()


def per_device(
    activations, d_logits, block_owner, left_stat, right_stat, second_moment, left_root, right_root
):
    tokens, width = activations.shape
    blocks = block_owner.shape[0]
    half = width // 2
    indices = jnp.arange(blocks, dtype=jnp.int32)
    owned = jnp.sum(jnp.where(block_owner[None, :] == indices[:, None], indices[None, :], 0), axis=1)
    rows = left_stat.shape[1]
    unit = 2 * rows
    vmem = pl.BlockSpec(memory_space=pltpu.VMEM)
    smem = pl.BlockSpec(memory_space=pltpu.SMEM)
    dma = pltpu.SemaphoreType.DMA
    stat = jax.ShapeDtypeStruct(left_stat.shape, F32)
    return pl.pallas_call(
        kernel,
        out_shape=(jax.ShapeDtypeStruct((blocks, rows, width), BF16), stat, stat, stat),
        in_specs=[smem, smem, vmem, pl.BlockSpec(memory_space=pl.ANY)] + [vmem] * 5,
        out_specs=(vmem,) * 4,
        scratch_shapes=[
            pltpu.VMEM((blocks, tokens, d_logits.shape[1] // blocks), BF16),
            pltpu.VMEM((blocks, tokens, d_logits.shape[1] // blocks), BF16),
            pltpu.VMEM((tokens, half), BF16),
            pltpu.VMEM((64, unit, half), F32),
            pltpu.VMEM((2, 4, 8, unit, half), F32),
            pltpu.VMEM((8, unit, half), F32),
            pltpu.VMEM((2, NL, 2, NX, rows, half), F32),
            pltpu.VMEM((NL, 2, NX, rows, width), F32),
            pltpu.VMEM((2, width, half), BF16),
            pltpu.VMEM((2, width, half), BF16),
            pltpu.VMEM((width, width), BF16),
            pltpu.VMEM((width, width), BF16),
            pltpu.VMEM((128, width), F32),
            pltpu.VMEM((32, 2, 128), F32),
            pltpu.VMEM((blocks, rows, width), BF16),
            dma, dma((2,)), dma((2,)),
            dma((2, 4, PIECES)), dma((2, 4, PIECES)),
            dma((8,)), dma((8,)),
            dma((2, 34)), dma((2, 2, NL, NX)),
            dma, dma,
            dma((15,)), dma((16,)),
        ],
        compiler_params=pltpu.CompilerParams(
            collective_id=0, has_side_effects=True, vmem_limit_bytes=40 * 2**20
        ),
    )(block_owner, owned, activations, d_logits, left_stat, right_stat, second_moment, left_root, right_root)


def solution(mesh):
    shards = P("dp", ("seq", "tensor"), None)
    return jax.shard_map(
        per_device,
        mesh=mesh,
        in_specs=(P(("dp", "seq"), None), P(("dp", "seq"), "tensor"), P()) + (shards,) * 5,
        out_specs=(P(None, ("seq", "tensor"), None), shards, shards, shards),
        check_vma=False,
    )
```

time: 537 us -> 86.6 us (0.16); the launches traced: 527 us -> 86 us
  waiting for transfers between devices: 379 us -> 0 us
  blocking collectives: 114 us -> 0 us
  Pallas kernels: 0 us -> 76 us
  between operations: 15.3 us -> 0.66 us
  matrix products: 10.7 us -> 0 us
    reduce_scatter x1 -> x0, waiting for transfers between devices: 202 us -> none  [per_device(): lax.psum_scatter(gradient_rows(by_owner, activations), ('dp', 'seq'), sca...]
    all_gather x2 -> x0, waiting for transfers between devices: 176 us -> none  [the longest x1 88.5 us: per_device(): slab_rows = lax.all_gather(grad_slab, ('seq', 'tensor'), axis=0, tiled=True)]
    pallas_call x0 -> x1, Pallas kernels: none -> 76 us  [per_device(): pl.pallas_call(kernel, out_shape=(jax.ShapeDtypeStruct((blocks, rows, wid...]
    psum x1 -> x0, blocking collectives: 67.3 us -> none  [per_device(): adam_total = lax.psum(adam_part, ('seq', 'tensor'))]
    all_gather x1 -> x0, blocking collectives: 46.3 us -> none  [per_device(): gathered = lax.all_gather(update_rows[None], 'dp', axis=0, tiled=True)]
    dot_general x5 -> x0, matrix products: 10.7 us -> none  [the longest x1 2.64 us: gradient_rows(): lax.dot_general(logit_columns, activations, (((0,), (0,)), ((), ())), pre...]
    unnamed x15 -> x20, local copies, waits for them, and re-layouts: 1.51 us -> 8.51 us
  transfers between devices with their start and end apart: 3 -> 0, of which waited for: 3 -> 0; matrix products, arithmetic and copies ran while one was open for 1% -> 0% of each run, Pallas kernels for 0% -> 0%
where the time goes in v1:
time: 86.6 us; the launch traced here: 86 us
  Pallas kernels  76 us (88%)
  local copies, waits for them, and re-layouts  8.51 us (10%)
    pallas_call x1, Pallas kernels, per_device(): pl.pallas_call(kernel, out_shape=(jax.ShapeDtypeStruct((blocks, rows, wid...  76 us
    unnamed x20, local copies, waits for them, and re-layouts  8.51 us

profile of v1, /device:TPU:1, one launch (start us, length us, event | category | flops | bytes accessed | tf_op | source)
XLA Modules:
  0.0 86.0 jit_solution(16396843727149237607)
XLA Ops:
  0.6 0.0 copy-start.7
  0.6 0.8 select_reduce_fusion.owned_ref
  1.5 0.0 copy-done.7
  1.5 0.0 copy-start
  1.5 1.2 %copy-done = bf16[256,2048]{1,0:T(8,128)(2,1)S(1)} copy-done((bf16[256,2048]{1,0:T(8,128)(2,1)S(1)}, bf16[256,2048]{1,0:T(8,128)(2,1)}, u32[]{:S(2)}) %copy-start) | copy-done | bytes 1048600
  2.7 0.0 copy-start.1
  2.7 0.9 %copy-done.1 = bf16[256,512]{1,0:T(8,128)(2,1)S(1)} copy-done((bf16[256,512]{1,0:T(8,128)(2,1)S(1)}, bf16[256,512]{1,0:T(8,128)(2,1)}, u32[]{:S(2)}) %copy-start.1) | copy-done | bytes 262168
  3.7 0.0 copy-start.2
  3.7 0.8 copy-done.2
  4.4 0.0 copy-start.3
  4.4 0.8 copy-done.3
  5.2 0.0 copy-start.4
  5.2 0.8 copy-done.4
  5.9 0.0 copy-start.5
  5.9 0.8 copy-done.5
  6.7 0.0 copy-start.6
  6.7 0.8 copy-done.6
  7.4 76.0 %shard_map.111 = (bf16[16,16,512]{2,1,0:T(8,128)(2,1)S(1)}, f32[1,16,512]{2,1,0:T(8,128)S(1)}, f32[1,16,512]{2,1,0:T(8,128)S(1)}, f32[1,16,512]{2,1,0:T(8,128)S(1)}) custom-call(s32[16]{0:T(128)S(1)} %copy-done.7, s32[16]{0:T(128)S(1)} %select_reduce_fusion.owned_ref, bf16[256,512]{1,0:T(8,128)(2,1)S(1)} %copy-done.1, bf16[256,2048]{1,0:T(8,128)(2,1)S(1)} %copy-done, ...), custom_call_target="tpu_custom_call" | custom-call | tf_op jit(solution)/shard_map/pallas_call | solution.py:399
  83.5 0.7 copy.16
  84.2 0.6 copy.17
  84.8 0.6 copy.18
  85.4 0.6 copy.19
Async XLA Ops:
  0.6 0.8 copy-start.7
  1.5 1.2 %copy-start = (bf16[256,2048]{1,0:T(8,128)(2,1)S(1)}, bf16[256,2048]{1,0:T(8,128)(2,1)}, u32[]{:S(2)}) copy-start(bf16[256,2048]{1,0:T(8,128)(2,1)} %logit_ref.1) | copy-start | bytes 3145732
  2.7 0.9 %copy-start.1 = (bf16[256,512]{1,0:T(8,128)(2,1)S(1)}, bf16[256,512]{1,0:T(8,128)(2,1)}, u32[]{:S(2)}) copy-start(bf16[256,512]{1,0:T(8,128)(2,1)} %acts_ref.1) | copy-start | bytes 786436
  3.7 0.8 copy-start.2
  4.4 0.8 copy-start.3
  5.2 0.8 copy-start.4
  5.9 0.8 copy-start.5
  6.7 0.8 copy-start.6

commit v2 on v1

--- a/solution.py
+++ b/solution.py
@@ -39,10 +39,10 @@
 
 
 def kernel(
-    owner_ref, owned_ref, acts_ref, logit_ref, left_ref, right_ref, moment_ref, lroot_ref, rroot_ref,
-    update_out, left_out, right_out, moment_out,
-    logit_own, logit_other, acts_other, part, ring_in, axis_in, grad, rroot, grad_hi, grad_lo,
-    rroot_hi, rroot_lo, columns, norms, updates,
+    owned_ref, acts_hbm, logit_ref, left_hbm, right_hbm, moment_hbm, lroot_hbm, rroot_hbm,
+    updates, left_out, right_out, moment_out,
+    acts_ref, left_ref, right_ref, moment_ref, lroot_ref, logit_own, logit_other, acts_other, part, ring_in, axis_in, grad, rroot, grad_hi, grad_lo,
+    rroot_hi, rroot_lo, columns, norms,
     load_done, ex_send, ex_recv, ring_send, ring_recv, axis_send, axis_recv, gather_send, gather_recv,
     norm_send, norm_recv, update_send, update_recv,
 ):
@@ -53,6 +53,7 @@
     yl, c = seq // 2, seq % 2
     y = yh * NL + yl
     half = acts_ref.shape[1] // 2
+    pending = []
 
     def at_yz(y_to, z_to):
         return (z_to * 2 + y_to // NL, (y_to % NL) * 2 + c, x)
@@ -74,9 +75,23 @@
     ring_prev = on_first((i + 7) % 8)
     x_next, x_prev, x_far = (x + 1) % NX, (x + 3) % NX, (x + 2) % NX
 
-    for b in range(owner_ref.shape[0]):
-        band = logit_ref.shape[1] // owner_ref.shape[0]
-        pltpu.make_async_copy(logit_ref.at[:, pl.ds(b * band, band)], logit_own.at[b], load_done).start()
+    acts_load = pltpu.make_async_copy(acts_hbm, acts_ref, load_done.at[1])
+    rroot_load = pltpu.make_async_copy(rroot_hbm.at[0], rroot.at[yl, c, x], load_done.at[2])
+    stat_loads = [
+        pltpu.make_async_copy(source, target, load_done.at[3 + k])
+        for k, (source, target) in enumerate(
+            ((left_hbm, left_ref), (right_hbm, right_ref), (moment_hbm, moment_ref), (lroot_hbm, lroot_ref))
+        )
+    ]
+    rroot_load.start()
+    acts_load.start()
+    blocks = owned_ref.shape[0]
+    band = logit_ref.shape[1] // blocks
+    for b in range(blocks):
+        pltpu.make_async_copy(logit_ref.at[:, pl.ds(b * band, band)], logit_own.at[b], load_done.at[0]).start()
+
+    for load in stat_loads:
+        load.start()
 
     barrier = pltpu.get_barrier_semaphore()
 
@@ -104,11 +119,9 @@
             device_id=device, device_id_type=MESH,
         )
 
-    blocks = owner_ref.shape[0]
-    band = logit_ref.shape[1] // blocks
     exchange = [
         remote(
-            acts_ref.at[:, pl.ds(pl.multiple_of((1 - c) * half, half), half)],
+            acts_hbm.at[:, pl.ds(pl.multiple_of((1 - c) * half, half), half)],
             acts_other, ex_send.at[0], ex_recv.at[0], sibling,
         )
     ]
@@ -118,72 +131,75 @@
         remote(strip, logit_other.at[b], ex_send.at[1], ex_recv.at[1], sibling).start()
     exchange.append(remote(logit_other, logit_other, ex_send.at[1], ex_recv.at[1], sibling))
 
-    def gather(which, slab):
-        sent = []
-
-        def arrive(q, core, column):
-            place = slab(q, core, column)
-            remote(
-                place, place, gather_send.at[which, 0], gather_recv.at[which, core, q, column], sibling
-            ).wait_recv()
+    def gather(which, slab, band_of):
+        count = [0]
+
+        def describe(place, k, core, q, column, device):
+            return remote(
+                place, place, gather_send.at[which, k], gather_recv.at[which, core, q, column], device
+            )
+
+        def arrive(q, column):
+            describe(slab(q, c, column), 0, c, q, column, sibling).wait_recv()
+
+        def launch(place, q, column, device):
+            copy = describe(place, count[0], c, q, column, device)
+            count[0] += 1
+            copy.start()
+            pending.append(copy)
 
         def push(q, column, device):
-            place = slab(q, c, column)
-            copy = remote(
-                place, place, gather_send.at[which, len(sent)],
-                gather_recv.at[which, c, q, column], device,
-            )
-            copy.start()
-            sent.append(copy)
+            launch(slab(q, c, column), q, column, device)
+
+        def share(q):
+            launch(band_of(q, c), q, 0, sibling)
 
         to_next, to_prev = in_group(yl, c, x_next), in_group(yl, c, x_prev)
 
+        def around(k):
+            return (yl, yl + 1 - 2 * (yl % 2), (yl + 2) % NL, NL - 1 - yl)[k]
+
         def begin():
+            for dy in range(1, NL):
+                push(yl, x, in_group(around(dy), c, x))
             push(yl, x, to_next)
             push(yl, x, to_prev)
+
+        def middle():
+            arrive(yl, x_prev)
+            push(yl, x_prev, to_next)
             for dy in range(1, NL):
-                push(yl, x, in_group((yl + dy) % NL, c, x))
-            push(yl, x, sibling)
-
-        def middle():
-            arrive(yl, c, x_prev)
-            push(yl, x_prev, to_next)
-            push(yl, x_prev, sibling)
-            arrive(yl, c, x_next)
-            push(yl, x_next, sibling)
-            for dy in range(1, NL):
-                q = (yl + NL - dy) % NL
-                arrive(q, c, x)
-                push(q, x, to_next)
-                push(q, x, to_prev)
-                push(q, x, sibling)
+                arrive(around(dy), x)
+                push(around(dy), x, to_next)
+                push(around(dy), x, to_prev)
 
         def late():
-            for dy in range(1, NL):
-                q = (yl + NL - dy) % NL
-                arrive(q, c, x_prev)
-                if dy == 1:
-                    push(q, x_prev, to_next)
-                push(q, x_prev, sibling)
-                arrive(q, c, x_next)
-                if dy >= 2:
-                    push(q, x_next, to_prev)
-                push(q, x_next, sibling)
+            arrive(around(1), x_prev)
+            push(around(1), x_prev, to_next)
+            for dy in (2, 3):
+                arrive(around(dy), x_next)
+                push(around(dy), x_next, to_prev)
 
         def end():
             for dy in range(NL):
-                q = (yl + NL - dy) % NL
-                arrive(q, c, x_far)
-                push(q, x_far, sibling)
-            for dx in range(NX):
-                for dy in range(NL):
-                    arrive((yl + dy) % NL, 1 - c, (x + dx) % NX)
-
-        return begin, middle, late, end, sent
-
-    rroot[yl, c, x] = rroot_ref[0]
-    r_begin, r_middle, r_late, r_end, r_sent = gather(0, lambda q, core, column: rroot.at[q, core, column])
-    g_begin, g_middle, g_late, g_end, g_sent = gather(1, lambda q, core, column: grad.at[core, q, :, column])
+                q = around(dy)
+                arrive(q, x_far)
+                arrive(q, x_next if dy < 2 else x_prev)
+                share(q)
+
+        def finish():
+            for q in range(NL):
+                describe(band_of(q, 1 - c), 0, 1 - c, q, 0, sibling).wait_recv()
+
+        return begin, middle, late, end, finish
+
+    rroot_load.wait()
+    r_begin, r_middle, r_late, r_end, r_finish = gather(
+        0, lambda q, core, column: rroot.at[q, core, column], lambda q, core: rroot.at[q, core]
+    )
+    g_begin, g_middle, g_late, g_end, g_finish = gather(
+        1, lambda q, core, column: grad.at[core, q, :, column], lambda q, core: grad.at[core, q]
+    )
     r_begin()
 
     unit = band // NL
@@ -191,8 +207,6 @@
     def place(d, q):
         row = (d % 2) * NL + q
         return (1 - c) * ((d // 2) * 8 + row) + c * (row * 8 + d // 2)
-
-    acts_own = acts_ref[:, pl.ds(pl.multiple_of(c * half, half), half)]
 
     def own_block(d, carry):
         rows = dot_tn(logit_own[owned_ref[d]], acts_own)
@@ -200,11 +214,13 @@
             part[place(d, q)] = rows[q * unit : (q + 1) * unit]
         return carry
 
-    pltpu.make_async_copy(logit_own, logit_own, load_done).wait()
-    lax.fori_loop(0, blocks, own_block, 0)
-    r_middle()
+    pltpu.make_async_copy(logit_own, logit_own, load_done.at[0]).wait()
+    acts_load.wait()
+    acts_own = acts_ref[:, pl.ds(pl.multiple_of(c * half, half), half)]
+    lax.fori_loop(0, blocks, own_block, 0, unroll=4)
     for copy in exchange:
         copy.wait_recv()
+    pending.extend(exchange)
 
     acts_rest = acts_other[...]
 
@@ -215,7 +231,7 @@
             part[spot] = part[spot] + rows[q * unit : (q + 1) * unit]
         return carry
 
-    lax.fori_loop(0, blocks, other_block, 0)
+    lax.fori_loop(0, blocks, other_block, 0, unroll=4)
 
     def chunk(way, step):
         return (i + 4 - step) % 8 if way == 0 else (i + 4 + step) % 8
@@ -236,21 +252,30 @@
         rows = pl.ds(spot * 8 + 2 * piece, 2)
         part[rows] = part[rows] + ring_in[way, step, pl.ds(2 * piece, 2)]
 
+    def ring_send_off(way, step, piece):
+        copy = ring(way, step, piece)
+        copy.start()
+        pending.append(copy)
+
     for k in range(2):
         for way in range(2):
-            ring(way, 0, first_pieces(way)[k]).start()
+            ring_send_off(way, 0, first_pieces(way)[k])
     for k in range(2):
         for way in range(2):
-            ring(way, 1, PIECE_ORDER[way][k]).start()
-    r_late()
+            ring_send_off(way, 1, PIECE_ORDER[way][k])
+    r_middle()
     for step in range(1, 4):
+        if step == 2:
+            r_late()
+        if step == 3:
+            r_end()
         for k in range(PIECES):
             for way in range(2):
                 piece = PIECE_ORDER[way][k]
                 if step == 1 and k < 2:
                     continue
                 ring_add(chunk(way, step), way, step - 1, piece)
-                ring(way, step, piece).start()
+                ring_send_off(way, step, piece)
 
     def axis_copy(j):
         return remote(
@@ -267,7 +292,9 @@
                 def _():
                     axis_copy(j).start()
 
-    r_end()
+    for k in range(1, 8):
+        pending.append(axis_copy((me2 + k) % 8))
+    r_finish()
     value = rroot[...].reshape(rroot_hi.shape)
     rroot_hi[...], rroot_lo[...] = split(value)
 
@@ -282,8 +309,11 @@
     g_middle()
     g_late()
     g_end()
+    g_finish()
 
     own = jnp.concatenate([grad[0, yl, c, x], grad[1, yl, c, x]], axis=1)
+    for load in stat_loads:
+        load.wait()
     moment = 0.99 * moment_ref[0] + 0.01 * own * own
     moment_out[0] = moment
     adam = own / (jnp.sqrt(moment) + 1e-08)
@@ -352,6 +382,7 @@
         copy = update_copy(across, NZ - 1 + k, at_yz(y, (z + k) % NZ))
         copy.start()
         update_sent.append(copy)
+    pending.extend(update_sent)
 
     first = seq * (NX * count) + x * count
     lane = 128
@@ -365,21 +396,16 @@
     for k in range(1, NZ):
         for side_y in range(2):
             update_copy(((z + k) % NZ) * 2 + side_y, 0, sibling).wait_recv()
-    for b in range(blocks):
+    for copy in pending:
+        copy.wait_send()
+
+
+def deliver(owner_ref, updates, left, right, moment, update_out, left_out, right_out, moment_out):
+    for b in range(owner_ref.shape[0]):
         update_out[b] = updates[owner_ref[b]]
-
-    for copy in exchange:
-        copy.wait_send()
-    for way in range(2):
-        for piece in first_pieces(way):
-            ring(way, 0, piece).wait_send()
-        for step in range(1, 4):
-            for piece in range(PIECES):
-                ring(way, step, piece).wait_send()
-    for k in range(1, 8):
-        axis_copy((me2 + k) % 8).wait_send()
-    for copy in r_sent + g_sent + update_sent:
-        copy.wait_send()
+    left_out[...] = left[...]
+    right_out[...] = right[...]
+    moment_out[...] = moment[...]
 
 
 def per_device(
@@ -396,12 +422,17 @@
     smem = pl.BlockSpec(memory_space=pltpu.SMEM)
     dma = pltpu.SemaphoreType.DMA
     stat = jax.ShapeDtypeStruct(left_stat.shape, F32)
-    return pl.pallas_call(
+    updates, left, right, moment = pl.pallas_call(
         kernel,
         out_shape=(jax.ShapeDtypeStruct((blocks, rows, width), BF16), stat, stat, stat),
-        in_specs=[smem, smem, vmem, pl.BlockSpec(memory_space=pl.ANY)] + [vmem] * 5,
+        in_specs=[smem] + [pl.BlockSpec(memory_space=pltpu.HBM)] * 7,
         out_specs=(vmem,) * 4,
         scratch_shapes=[
+            pltpu.VMEM((tokens, width), BF16),
+            pltpu.VMEM(left_stat.shape, F32),
+            pltpu.VMEM(left_stat.shape, F32),
+            pltpu.VMEM(left_stat.shape, F32),
+            pltpu.VMEM(left_stat.shape, F32),
             pltpu.VMEM((blocks, tokens, d_logits.shape[1] // blocks), BF16),
             pltpu.VMEM((blocks, tokens, d_logits.shape[1] // blocks), BF16),
             pltpu.VMEM((tokens, half), BF16),
@@ -416,18 +447,23 @@
             pltpu.VMEM((width, width), BF16),
             pltpu.VMEM((128, width), F32),
             pltpu.VMEM((32, 2, 128), F32),
-            pltpu.VMEM((blocks, rows, width), BF16),
-            dma, dma((2,)), dma((2,)),
+            dma((7,)), dma((2,)), dma((2,)),
             dma((2, 4, PIECES)), dma((2, 4, PIECES)),
             dma((8,)), dma((8,)),
-            dma((2, 34)), dma((2, 2, NL, NX)),
+            dma((2, 24)), dma((2, 2, NL, NX)),
             dma, dma,
             dma((15,)), dma((16,)),
         ],
         compiler_params=pltpu.CompilerParams(
-            collective_id=0, has_side_effects=True, vmem_limit_bytes=40 * 2**20
+            collective_id=0, has_side_effects=True, vmem_limit_bytes=60 * 2**20
         ),
-    )(block_owner, owned, activations, d_logits, left_stat, right_stat, second_moment, left_root, right_root)
+    )(owned, activations, d_logits, left_stat, right_stat, second_moment, left_root, right_root)
+    return pl.pallas_call(
+        deliver,
+        out_shape=(jax.ShapeDtypeStruct(updates.shape, BF16), stat, stat, stat),
+        in_specs=[smem] + [vmem] * 4,
+        out_specs=(vmem,) * 4,
+    )(block_owner, updates, left, right, moment)
 
 
 def solution(mesh):

time: 86.6 us -> 75 us (0.87)
  local copies, waits for them, and re-layouts: 8.51 us -> 0 us
  Pallas kernels: 76 us -> 72.9 us
    unnamed x20 -> x0, local copies, waits for them, and re-layouts: 8.51 us -> none
    pallas_call x1, Pallas kernels: 76 us -> 71.2 us  [per_device(): pl.pallas_call(kernel, out_shape=(jax.ShapeDtypeStruct((blocks, rows, wid...]
    pallas_call x0 -> x1, Pallas kernels: none -> 1.74 us  [per_device(): pl.pallas_call(deliver, out_shape=(jax.ShapeDtypeStruct(updates.shape, BF...]
where the time goes in v2:
time: 75 us; the launch traced here: 74.8 us
  Pallas kernels  72.9 us (97%)
  other arithmetic  1.28 us (2%)
    pallas_call x1, Pallas kernels, per_device(): pl.pallas_call(kernel, out_shape=(jax.ShapeDtypeStruct((blocks, rows, wid...  71.2 us
    pallas_call x1, Pallas kernels, per_device(): pl.pallas_call(deliver, out_shape=(jax.ShapeDtypeStruct(updates.shape, BF...  1.74 us

profile of v2, /device:TPU:1, one launch (start us, length us, event | category | flops | bytes accessed | tf_op | source)
XLA Modules:
  0.0 74.8 jit_solution(7624601846060868608)
XLA Ops:
  0.6 1.3 %select_reduce_fusion.owned_ref = s32[16]{0:T(128)} fusion(s32[16]{0:T(128)} %owner_ref.1), kind=kLoop, calls=%fused_computation | loop fusion | flops 752 | bytes 128 | tf_op jit(solution)/shard_map/reduce_sum | solution.py:418
  1.9 71.2 %shard_map.111 = (bf16[16,16,512]{2,1,0:T(8,128)(2,1)}, f32[1,16,512]{2,1,0:T(8,128)}, f32[1,16,512]{2,1,0:T(8,128)}, f32[1,16,512]{2,1,0:T(8,128)}) custom-call(s32[16]{0:T(128)} %select_reduce_fusion.owned_ref, bf16[256,512]{1,0:T(8,128)(2,1)} %acts_hbm.1, bf16[256,2048]{1,0:T(8,128)(2,1)} %logit_ref.1, f32[1,16,512]{2,1,0:T(8,128)} %left_hbm.1, ...), custom_call_target="tpu_custom_call" | custom-call | tf_op jit(solution)/shard_map/pallas_call | solution.py:425
  73.1 1.7 %shard_map.112 = (bf16[16,16,512]{2,1,0:T(8,128)(2,1)}, f32[1,16,512]{2,1,0:T(8,128)}, f32[1,16,512]{2,1,0:T(8,128)}, f32[1,16,512]{2,1,0:T(8,128)}) custom-call(s32[16]{0:T(128)} %owner_ref.1, bf16[16,16,512]{2,1,0:T(8,128)(2,1)} %get-tuple-element.8.updates, f32[1,16,512]{2,1,0:T(8,128)} %get-tuple-element.9.left, f32[1,16,512]{2,1,0:T(8,128)} %get-tuple-element.10.right, ...), custom_call_target="tpu_custom_call" | custom-call | tf_op jit(solution)/shard_map/pallas_call | solution.py:461

commit v3 on v2

--- a/solution.py
+++ b/solution.py
@@ -14,6 +14,7 @@
 NL = 4
 NX = 4
 PIECES = 4
+FAR_FIRST = (4, 3, 5, 2, 6, 1, 7)
 PIECE_ORDER = ((2, 3, 0, 1), (0, 1, 2, 3))
 
 
@@ -41,10 +42,10 @@
 def kernel(
     owned_ref, acts_hbm, logit_ref, left_hbm, right_hbm, moment_hbm, lroot_hbm, rroot_hbm,
     updates, left_out, right_out, moment_out,
-    acts_ref, left_ref, right_ref, moment_ref, lroot_ref, logit_own, logit_other, acts_other, part, ring_in, axis_in, grad, rroot, grad_hi, grad_lo,
-    rroot_hi, rroot_lo, columns, norms,
+    acts_ref, left_ref, right_ref, moments, lroots, logit_own, logit_other, acts_other, part, ring_in, axis_in, grad, rroot, grad_hi, grad_lo,
+    rroot_hi, rroot_lo, columns, precond, adam_norms, norms,
     load_done, ex_send, ex_recv, ring_send, ring_recv, axis_send, axis_recv, gather_send, gather_recv,
-    norm_send, norm_recv, update_send, update_recv,
+    lroot_send, lroot_recv, adam_send, adam_recv, norm_send, norm_recv, update_send, update_recv,
 ):
     dp = lax.axis_index("dp")
     seq = lax.axis_index("seq")
@@ -80,11 +81,13 @@
     stat_loads = [
         pltpu.make_async_copy(source, target, load_done.at[3 + k])
         for k, (source, target) in enumerate(
-            ((left_hbm, left_ref), (right_hbm, right_ref), (moment_hbm, moment_ref), (lroot_hbm, lroot_ref))
+            ((left_hbm, left_ref), (right_hbm, right_ref), (moment_hbm.at[0], moments.at[c]))
         )
     ]
+    lroot_load = pltpu.make_async_copy(lroot_hbm.at[0], lroots.at[c, x], load_done.at[6])
     rroot_load.start()
     acts_load.start()
+    lroot_load.start()
     blocks = owned_ref.shape[0]
     band = logit_ref.shape[1] // blocks
     for b in range(blocks):
@@ -98,20 +101,17 @@
     def signal(device):
         pl.semaphore_signal(barrier, inc=1, device_id=device, device_id_type=MESH)
 
-    partners = 0
-    for dx in range(NX):
-        for dy in range(NL):
-            for dc in range(2):
-                if dx or dy or dc:
-                    signal(in_group((yl + dy) % NL, (c + dc) % 2, (x + dx) % NX))
-                    partners += 1
-    for k in range(NL):
-        signal(at_yz((1 - yh) * NL + k, z))
-        partners += 1
-    for k in range(1, NZ):
-        signal(at_yz(y, (z + k) % NZ))
-        partners += 1
-    pl.semaphore_wait(barrier, partners)
+    partners = [at_yz((1 - yh) * NL + k, z) for k in range(NL)]
+    partners += [at_yz(y, (z + k) % NZ) for k in FAR_FIRST]
+    for k in (3, 2, 1, 0):
+        yl_to = (yl, yl + 1 - 2 * (yl % 2), (yl + 2) % NL, NL - 1 - yl)[k]
+        for dx in (2, 1, 3, 0):
+            for dc in (1, 0):
+                if dx or k or dc:
+                    partners.append(in_group(yl_to, (c + dc) % 2, (x + dx) % NX))
+    for device in partners:
+        signal(device)
+    pl.semaphore_wait(barrier, len(partners))
 
     def remote(src, dst, send, recv, device):
         return pltpu.make_async_remote_copy(
@@ -129,6 +129,8 @@
     for b in range(blocks):
         strip = logit_ref.at[:, pl.ds(b * band, band)]
         remote(strip, logit_other.at[b], ex_send.at[1], ex_recv.at[1], sibling).start()
+    exchange.append(remote(moment_hbm.at[0], moments.at[c], ex_send.at[2], ex_recv.at[2], sibling))
+    exchange[1].start()
     exchange.append(remote(logit_other, logit_other, ex_send.at[1], ex_recv.at[1], sibling))
 
     def gather(which, slab, band_of):
@@ -154,59 +156,65 @@
         def share(q):
             launch(band_of(q, c), q, 0, sibling)
 
-        to_next, to_prev = in_group(yl, c, x_next), in_group(yl, c, x_prev)
+        columns_to = [in_group(yl, c, column) for column in (x_far, x_next, x_prev)]
 
         def around(k):
             return (yl, yl + 1 - 2 * (yl % 2), (yl + 2) % NL, NL - 1 - yl)[k]
 
         def begin():
-            for dy in range(1, NL):
-                push(yl, x, in_group(around(dy), c, x))
-            push(yl, x, to_next)
-            push(yl, x, to_prev)
+            for k in (3, 2, 1):
+                push(yl, x, in_group(around(k), c, x))
+            for device in columns_to:
+                push(yl, x, device)
 
         def middle():
-            arrive(yl, x_prev)
-            push(yl, x_prev, to_next)
-            for dy in range(1, NL):
-                arrive(around(dy), x)
-                push(around(dy), x, to_next)
-                push(around(dy), x, to_prev)
-
-        def late():
-            arrive(around(1), x_prev)
-            push(around(1), x_prev, to_next)
-            for dy in (2, 3):
-                arrive(around(dy), x_next)
-                push(around(dy), x_next, to_prev)
-
-        def end():
-            for dy in range(NL):
-                q = around(dy)
-                arrive(q, x_far)
-                arrive(q, x_next if dy < 2 else x_prev)
-                share(q)
+            for k in (1, 2, 3):
+                arrive(around(k), x)
+                for device in columns_to:
+                    push(around(k), x, device)
+
+        def late(k):
+            for column in (x_next, x_prev, x_far):
+                arrive(around(k), column)
+            share(around(k))
 
         def finish():
             for q in range(NL):
                 describe(band_of(q, 1 - c), 0, 1 - c, q, 0, sibling).wait_recv()
 
-        return begin, middle, late, end, finish
+        return begin, middle, late, finish
 
     rroot_load.wait()
-    r_begin, r_middle, r_late, r_end, r_finish = gather(
+    r_begin, r_middle, r_late, r_finish = gather(
         0, lambda q, core, column: rroot.at[q, core, column], lambda q, core: rroot.at[q, core]
     )
-    g_begin, g_middle, g_late, g_end, g_finish = gather(
+    g_begin, g_middle, g_late, g_finish = gather(
         1, lambda q, core, column: grad.at[core, q, :, column], lambda q, core: grad.at[core, q]
     )
     r_begin()
 
+    def lroot_copy(k, column, device):
+        return remote(
+            lroots.at[c, column], lroots.at[c, column], lroot_send.at[k], lroot_recv.at[0, column], device
+        )
+
+    def lroot_band(core):
+        return remote(lroots.at[core], lroots.at[core], lroot_send.at[3], lroot_recv.at[1, 0], sibling)
+
+    lroot_load.wait()
+    for k, column in enumerate((x_far, x_next, x_prev)):
+        copy = lroot_copy(k, x, in_group(yl, c, column))
+        copy.start()
+        pending.append(copy)
+
     unit = band // NL
 
     def place(d, q):
         row = (d % 2) * NL + q
         return (1 - c) * ((d // 2) * 8 + row) + c * (row * 8 + d // 2)
+
+    def ordered(n):
+        return (1 - c) * ((2 * (i + 4) + n) % 16) + c * (2 * (n % 8) + (yh + 1 + n // 8) % 2)
 
     def own_block(d, carry):
         rows = dot_tn(logit_own[owned_ref[d]], acts_own)
@@ -224,14 +232,14 @@
 
     acts_rest = acts_other[...]
 
-    def other_block(d, carry):
+    def other_block(n, carry):
+        d = ordered(n)
         rows = dot_tn(logit_other[owned_ref[d]], acts_rest)
         for q in range(NL):
             spot = place(d, q)
             part[spot] = part[spot] + rows[q * unit : (q + 1) * unit]
         return carry
 
-    lax.fori_loop(0, blocks, other_block, 0, unroll=4)
 
     def chunk(way, step):
         return (i + 4 - step) % 8 if way == 0 else (i + 4 + step) % 8
@@ -257,18 +265,27 @@
         copy.start()
         pending.append(copy)
 
+    lax.fori_loop(0, blocks // 2, other_block, 0, unroll=4)
     for k in range(2):
         for way in range(2):
             ring_send_off(way, 0, first_pieces(way)[k])
+    lax.fori_loop(blocks // 2, blocks, other_block, 0, unroll=4)
     for k in range(2):
         for way in range(2):
             ring_send_off(way, 1, PIECE_ORDER[way][k])
     r_middle()
     for step in range(1, 4):
         if step == 2:
-            r_late()
+            for column in (x_next, x_prev, x_far):
+                lroot_copy(0, column, sibling).wait_recv()
+            copy = lroot_band(c)
+            copy.start()
+            pending.append(copy)
+            r_late(0)
+            r_late(1)
         if step == 3:
-            r_end()
+            r_late(2)
+            r_late(3)
         for k in range(PIECES):
             for way in range(2):
                 piece = PIECE_ORDER[way][k]
@@ -295,6 +312,7 @@
     for k in range(1, 8):
         pending.append(axis_copy((me2 + k) % 8))
     r_finish()
+    lroot_band(1 - c).wait_recv()
     value = rroot[...].reshape(rroot_hi.shape)
     rroot_hi[...], rroot_lo[...] = split(value)
 
@@ -306,21 +324,55 @@
     grad[c, yl, :, x] = total.reshape(2, unit // 2, half)
 
     g_begin()
-    g_middle()
-    g_late()
-    g_end()
-    g_finish()
-
-    own = jnp.concatenate([grad[0, yl, c, x], grad[1, yl, c, x]], axis=1)
     for load in stat_loads:
         load.wait()
-    moment = 0.99 * moment_ref[0] + 0.01 * own * own
-    moment_out[0] = moment
-    adam = own / (jnp.sqrt(moment) + 1e-08)
-    adam_part = sum_all(adam * adam)
-
-    for s in range(2):
-        grad_hi[s], grad_lo[s] = split(grad[s].reshape(grad_hi.shape[1:]))
+
+    slab_grad = total.reshape(2, unit // 2, half)
+    slab_moment = moments[:, :, pl.ds(pl.multiple_of(c * half, half), half)]
+    slab_adam = slab_grad / (jnp.sqrt(0.99 * slab_moment + 0.01 * slab_grad * slab_grad) + 1e-08)
+    lanes = norms.shape[2]
+    rank = (yl * 2 + c) * NX + x
+    adam_norms[rank] = jnp.broadcast_to(sum_all((slab_adam * slab_adam).reshape(unit, half)), (1, lanes))
+    for k in range(NL):
+        for dx in range(NX):
+            for dc in range(2):
+                if dx or k or dc:
+                    remote(
+                        adam_norms.at[rank], adam_norms.at[rank], adam_send, adam_recv,
+                        in_group((yl + k) % NL, (c + dc) % 2, (x + dx) % NX),
+                    ).start()
+
+    count = lroots.shape[2]
+    chip_rows = lroots.shape[0] * lroots.shape[1] * count
+    lroot_hi, lroot_lo = split(lroots[...].reshape(chip_rows, lroots.shape[3]))
+    lroot_both = jnp.concatenate([lroot_hi, lroot_lo], axis=0)
+    g_middle()
+    for k in range(NL):
+        g_late(k)
+
+    def precond_half(s):
+        high, low = split(grad[s].reshape(grad_hi.shape[1:]))
+        grad_hi[s] = high
+        grad_lo[s] = low
+        wide = dot(lroot_both, high)
+        mixed = wide[:chip_rows] + (wide[chip_rows:] + dot(lroot_hi, low))
+        mixed_hi, mixed_lo = split(mixed)
+        span = pl.ds(pl.multiple_of(s * half, half), half)
+        wide = dot(jnp.concatenate([mixed_hi, mixed_lo], axis=0), rroot_hi[span])
+        return wide[:chip_rows] + (wide[chip_rows:] + dot(mixed_hi, rroot_lo[span]))
+
+    precond[...] = precond_half(c).reshape(precond.shape)
+    g_finish()
+    chip_precond = precond[...].reshape(chip_rows, 2 * half) + precond_half(1 - c)
+    precond[...] = chip_precond.reshape(precond.shape)
+
+    norms[yl] = jnp.broadcast_to(sum_all(chip_precond * chip_precond), (1, lanes))
+    for k in (3, 2, 1):
+        yl_to = (yl, yl + 1 - 2 * (yl % 2), (yl + 2) % NL, NL - 1 - yl)[k]
+        remote(norms.at[yl], norms.at[yl], norm_send, norm_recv, in_group(yl_to, c, x)).start()
+
+    own = jnp.concatenate([grad[0, yl, c, x], grad[1, yl, c, x]], axis=1)
+    moment_out[0] = 0.99 * moments[c] + 0.01 * own * own
 
     def times_grad(value):
         rows = value.shape[0]
@@ -332,27 +384,6 @@
             out.append(wide[:rows] + (wide[rows:] + dot(high, grad_lo[s])))
         return jnp.concatenate(out, axis=1)
 
-    mixed = times_grad(lroot_ref[0])
-    mixed_hi, mixed_lo = split(mixed)
-    wide = dot(jnp.concatenate([mixed_hi, mixed_lo], axis=0), rroot_hi[...])
-    count = mixed.shape[0]
-    precond = wide[:count] + (wide[count:] + dot(mixed_hi, rroot_lo[...]))
-    precond_part = sum_all(precond * precond)
-
-    lanes = norms.shape[2]
-    rank = (yl * 2 + c) * NX + x
-    norms[rank] = jnp.concatenate(
-        [jnp.broadcast_to(adam_part, (1, lanes)), jnp.broadcast_to(precond_part, (1, lanes))], axis=0
-    )
-    for dx in range(NX):
-        for dy in range(NL):
-            for dc in range(2):
-                if dx or dy or dc:
-                    remote(
-                        norms.at[rank], norms.at[rank], norm_send, norm_recv,
-                        in_group((yl + dy) % NL, (c + dc) % 2, (x + dx) % NX),
-                    ).start()
-
     own_hi, own_lo = split(own)
     both = jnp.concatenate([own_hi, own_lo], axis=0)
     outer = 0.95 * left_ref[0]
@@ -362,23 +393,26 @@
         outer = outer + (wide[:count] + (wide[count:] + dot_nt(own_hi[:, span], grad_lo[s])))
     left_out[0] = outer
 
-    everyone = norms.at[pl.ds(0, norms.shape[0] - 1)]
-    remote(everyone, everyone, norm_send, norm_recv, sibling).wait()
-    sums = jnp.sum(norms[...], axis=0)
-    scale = jnp.sqrt(sums[0:1, 0:1]) / (jnp.sqrt(sums[1:2, 0:1]) + 1e-06)
-    updates[dp] = (scale * precond).astype(BF16)
+    everyone = adam_norms.at[pl.ds(0, adam_norms.shape[0] - 1)]
+    remote(everyone, everyone, adam_send, adam_recv, sibling).wait()
+    others = norms.at[pl.ds(0, NL - 1)]
+    remote(others, others, norm_send, norm_recv, sibling).wait()
+    adam_total = jnp.sum(adam_norms[...], axis=0)
+    precond_total = jnp.sum(norms[...], axis=0)
+    scale = jnp.sqrt(adam_total[:, 0:1]) / (jnp.sqrt(precond_total[:, 0:1]) + 1e-06)
+    updates[dp] = (scale * precond[c * NX + x]).astype(BF16)
 
     def update_copy(d, k, device):
         return remote(updates.at[d], updates.at[d], update_send.at[k], update_recv.at[d], device)
 
     across = z * 2 + (1 - yh)
     update_sent = [update_copy(dp, 0, at_yz((1 - yh) * NL + yl, z))]
-    for k in range(1, NZ):
+    for k in FAR_FIRST:
         update_sent.append(update_copy(dp, k, at_yz(y, (z + k) % NZ)))
     for copy in update_sent:
         copy.start()
     update_copy(across, 0, sibling).wait_recv()
-    for k in range(1, NZ):
+    for k in FAR_FIRST:
         copy = update_copy(across, NZ - 1 + k, at_yz(y, (z + k) % NZ))
         copy.start()
         update_sent.append(copy)
@@ -431,8 +465,8 @@
             pltpu.VMEM((tokens, width), BF16),
             pltpu.VMEM(left_stat.shape, F32),
             pltpu.VMEM(left_stat.shape, F32),
-            pltpu.VMEM(left_stat.shape, F32),
-            pltpu.VMEM(left_stat.shape, F32),
+            pltpu.VMEM((2, rows, width), F32),
+            pltpu.VMEM((2, NX, rows, width), F32),
             pltpu.VMEM((blocks, tokens, d_logits.shape[1] // blocks), BF16),
             pltpu.VMEM((blocks, tokens, d_logits.shape[1] // blocks), BF16),
             pltpu.VMEM((tokens, half), BF16),
@@ -446,11 +480,15 @@
             pltpu.VMEM((width, width), BF16),
             pltpu.VMEM((width, width), BF16),
             pltpu.VMEM((128, width), F32),
-            pltpu.VMEM((32, 2, 128), F32),
-            dma((7,)), dma((2,)), dma((2,)),
+            pltpu.VMEM((2 * NX, rows, width), F32),
+            pltpu.VMEM((32, 1, 128), F32),
+            pltpu.VMEM((NL, 1, 128), F32),
+            dma((7,)), dma((3,)), dma((3,)),
             dma((2, 4, PIECES)), dma((2, 4, PIECES)),
             dma((8,)), dma((8,)),
             dma((2, 24)), dma((2, 2, NL, NX)),
+            dma((4,)), dma((2, NX)),
+            dma, dma,
             dma, dma,
             dma((15,)), dma((16,)),
         ],

time: 75 us -> 70.6 us (0.941)
  Pallas kernels: 72.9 us -> 68.3 us
    pallas_call x1, Pallas kernels: 71.2 us -> 66.6 us  [per_device(): pl.pallas_call(kernel, out_shape=(jax.ShapeDtypeStruct((blocks, rows, wid...]
where the time goes in v3:
time: 70.6 us; the launch traced here: 70.3 us
  Pallas kernels  68.3 us (97%)
  other arithmetic  1.28 us (2%)
    pallas_call x1, Pallas kernels, per_device(): pl.pallas_call(kernel, out_shape=(jax.ShapeDtypeStruct((blocks, rows, wid...  66.6 us
    pallas_call x1, Pallas kernels, per_device(): pl.pallas_call(deliver, out_shape=(jax.ShapeDtypeStruct(updates.shape, BF...  1.74 us

profile of v3, /device:TPU:1, one launch (start us, length us, event | category | flops | bytes accessed | tf_op | source)
XLA Modules:
  0.0 70.3 jit_solution(12069210988370263711)
XLA Ops:
  0.6 1.3 %select_reduce_fusion.owned_ref = s32[16]{0:T(128)} fusion(s32[16]{0:T(128)} %owner_ref.1), kind=kLoop, calls=%fused_computation | loop fusion | flops 752 | bytes 128 | tf_op jit(solution)/shard_map/reduce_sum | solution.py:452
  1.9 66.6 %shard_map.111 = (bf16[16,16,512]{2,1,0:T(8,128)(2,1)}, f32[1,16,512]{2,1,0:T(8,128)}, f32[1,16,512]{2,1,0:T(8,128)}, f32[1,16,512]{2,1,0:T(8,128)}) custom-call(s32[16]{0:T(128)} %select_reduce_fusion.owned_ref, bf16[256,512]{1,0:T(8,128)(2,1)} %acts_hbm.1, bf16[256,2048]{1,0:T(8,128)(2,1)} %logit_ref.1, f32[1,16,512]{2,1,0:T(8,128)} %left_hbm.1, ...), custom_call_target="tpu_custom_call" | custom-call | tf_op jit(solution)/shard_map/pallas_call | solution.py:459
  68.5 1.7 %shard_map.112 = (bf16[16,16,512]{2,1,0:T(8,128)(2,1)}, f32[1,16,512]{2,1,0:T(8,128)}, f32[1,16,512]{2,1,0:T(8,128)}, f32[1,16,512]{2,1,0:T(8,128)}) custom-call(s32[16]{0:T(128)} %owner_ref.1, bf16[16,16,512]{2,1,0:T(8,128)(2,1)} %get-tuple-element.8.updates, f32[1,16,512]{2,1,0:T(8,128)} %get-tuple-element.9.left, f32[1,16,512]{2,1,0:T(8,128)} %get-tuple-element.10.right, ...), custom_call_target="tpu_custom_call" | custom-call | tf_op jit(solution)/shard_map/pallas_call | solution.py:499

commit v4 on v3

--- a/solution.py
+++ b/solution.py
@@ -40,9 +40,9 @@
 
 
 def kernel(
-    owned_ref, acts_hbm, logit_ref, left_hbm, right_hbm, moment_hbm, lroot_hbm, rroot_hbm,
+    owner_ref, acts_hbm, logit_ref, left_hbm, right_hbm, moment_hbm, lroot_hbm, rroot_hbm,
     updates, left_out, right_out, moment_out,
-    acts_ref, left_ref, right_ref, moments, lroots, logit_own, logit_other, acts_other, part, ring_in, axis_in, grad, rroot, grad_hi, grad_lo,
+    owned_ref, acts_ref, left_ref, right_ref, moments, lroots, logit_own, logit_other, acts_other, part, ring_in, axis_in, grad, rroot, grad_hi, grad_lo,
     rroot_hi, rroot_lo, columns, precond, adam_norms, norms,
     load_done, ex_send, ex_recv, ring_send, ring_recv, axis_send, axis_recv, gather_send, gather_recv,
     lroot_send, lroot_recv, adam_send, adam_recv, norm_send, norm_recv, update_send, update_recv,
@@ -88,7 +88,7 @@
     rroot_load.start()
     acts_load.start()
     lroot_load.start()
-    blocks = owned_ref.shape[0]
+    blocks = owner_ref.shape[0]
     band = logit_ref.shape[1] // blocks
     for b in range(blocks):
         pltpu.make_async_copy(logit_ref.at[:, pl.ds(b * band, band)], logit_own.at[b], load_done.at[0]).start()
@@ -103,12 +103,8 @@
 
     partners = [at_yz((1 - yh) * NL + k, z) for k in range(NL)]
     partners += [at_yz(y, (z + k) % NZ) for k in FAR_FIRST]
-    for k in (3, 2, 1, 0):
-        yl_to = (yl, yl + 1 - 2 * (yl % 2), (yl + 2) % NL, NL - 1 - yl)[k]
-        for dx in (2, 1, 3, 0):
-            for dc in (1, 0):
-                if dx or k or dc:
-                    partners.append(in_group(yl_to, (c + dc) % 2, (x + dx) % NX))
+    partners += [in_group((yl + k) % NL, c, x) for k in range(1, NL)]
+    partners += [in_group(yl, c, column) for column in (x_far, x_next, x_prev)] + [sibling]
     for device in partners:
         signal(device)
     pl.semaphore_wait(barrier, len(partners))
@@ -217,7 +213,13 @@
         return (1 - c) * ((2 * (i + 4) + n) % 16) + c * (2 * (n % 8) + (yh + 1 + n // 8) % 2)
 
     def own_block(d, carry):
-        rows = dot_tn(logit_own[owned_ref[d]], acts_own)
+        b = jnp.int32(0)
+        for k in range(1, blocks):
+            apart = owner_ref[k] - d
+            b = b + k * lax.shift_right_logical(blocks * blocks - apart * apart, jnp.int32(8))
+        b = lax.rem(b, jnp.int32(blocks))
+        owned_ref[d] = b
+        rows = dot_tn(logit_own[b], acts_own)
         for q in range(NL):
             part[place(d, q)] = rows[q * unit : (q + 1) * unit]
         return carry
@@ -331,24 +333,32 @@
     slab_moment = moments[:, :, pl.ds(pl.multiple_of(c * half, half), half)]
     slab_adam = slab_grad / (jnp.sqrt(0.99 * slab_moment + 0.01 * slab_grad * slab_grad) + 1e-08)
     lanes = norms.shape[2]
-    rank = (yl * 2 + c) * NX + x
-    adam_norms[rank] = jnp.broadcast_to(sum_all((slab_adam * slab_adam).reshape(unit, half)), (1, lanes))
-    for k in range(NL):
-        for dx in range(NX):
-            for dc in range(2):
-                if dx or k or dc:
-                    remote(
-                        adam_norms.at[rank], adam_norms.at[rank], adam_send, adam_recv,
-                        in_group((yl + k) % NL, (c + dc) % 2, (x + dx) % NX),
-                    ).start()
-
+
+    def adam_copy(level, place, device):
+        spot = adam_norms.at[level, place]
+        return remote(spot, spot, adam_send.at[level], adam_recv.at[level], device)
+
+    def adam_sum(level, others):
+        several = adam_norms.at[level, pl.ds(0, others)]
+        remote(several, several, adam_send.at[level], adam_recv.at[level], sibling).wait()
+        return jnp.sum(adam_norms[level, 0 : others + 1], axis=0)
+
+    adam_norms[0, c] = jnp.broadcast_to(sum_all((slab_adam * slab_adam).reshape(unit, half)), (1, lanes))
+    adam_copy(0, c, sibling).start()
     count = lroots.shape[2]
     chip_rows = lroots.shape[0] * lroots.shape[1] * count
     lroot_hi, lroot_lo = split(lroots[...].reshape(chip_rows, lroots.shape[3]))
     lroot_both = jnp.concatenate([lroot_hi, lroot_lo], axis=0)
+    adam_norms[1, x] = adam_sum(0, 1)
+    for column in (x_far, x_next, x_prev):
+        adam_copy(1, x, in_group(yl, c, column)).start()
     g_middle()
+    adam_norms[2, yl] = adam_sum(1, NX - 1)
+    for k in range(1, NL):
+        adam_copy(2, yl, in_group((yl + k) % NL, c, x)).start()
     for k in range(NL):
         g_late(k)
+    adam_total = adam_sum(2, NL - 1)
 
     def precond_half(s):
         high, low = split(grad[s].reshape(grad_hi.shape[1:]))
@@ -393,11 +403,8 @@
         outer = outer + (wide[:count] + (wide[count:] + dot_nt(own_hi[:, span], grad_lo[s])))
     left_out[0] = outer
 
-    everyone = adam_norms.at[pl.ds(0, adam_norms.shape[0] - 1)]
-    remote(everyone, everyone, adam_send, adam_recv, sibling).wait()
     others = norms.at[pl.ds(0, NL - 1)]
     remote(others, others, norm_send, norm_recv, sibling).wait()
-    adam_total = jnp.sum(adam_norms[...], axis=0)
     precond_total = jnp.sum(norms[...], axis=0)
     scale = jnp.sqrt(adam_total[:, 0:1]) / (jnp.sqrt(precond_total[:, 0:1]) + 1e-06)
     updates[dp] = (scale * precond[c * NX + x]).astype(BF16)
@@ -448,8 +455,6 @@
     tokens, width = activations.shape
     blocks = block_owner.shape[0]
     half = width // 2
-    indices = jnp.arange(blocks, dtype=jnp.int32)
-    owned = jnp.sum(jnp.where(block_owner[None, :] == indices[:, None], indices[None, :], 0), axis=1)
     rows = left_stat.shape[1]
     unit = 2 * rows
     vmem = pl.BlockSpec(memory_space=pltpu.VMEM)
@@ -462,6 +467,7 @@
         in_specs=[smem] + [pl.BlockSpec(memory_space=pltpu.HBM)] * 7,
         out_specs=(vmem,) * 4,
         scratch_shapes=[
+            pltpu.SMEM((blocks,), jnp.int32),
             pltpu.VMEM((tokens, width), BF16),
             pltpu.VMEM(left_stat.shape, F32),
             pltpu.VMEM(left_stat.shape, F32),
@@ -481,21 +487,21 @@
             pltpu.VMEM((width, width), BF16),
             pltpu.VMEM((128, width), F32),
             pltpu.VMEM((2 * NX, rows, width), F32),
-            pltpu.VMEM((32, 1, 128), F32),
+            pltpu.VMEM((3, NX, 1, 128), F32),
             pltpu.VMEM((NL, 1, 128), F32),
             dma((7,)), dma((3,)), dma((3,)),
             dma((2, 4, PIECES)), dma((2, 4, PIECES)),
             dma((8,)), dma((8,)),
             dma((2, 24)), dma((2, 2, NL, NX)),
             dma((4,)), dma((2, NX)),
-            dma, dma,
+            dma((3,)), dma((3,)),
             dma, dma,
             dma((15,)), dma((16,)),
         ],
         compiler_params=pltpu.CompilerParams(
             collective_id=0, has_side_effects=True, vmem_limit_bytes=60 * 2**20
         ),
-    )(owned, activations, d_logits, left_stat, right_stat, second_moment, left_root, right_root)
+    )(block_owner, activations, d_logits, left_stat, right_stat, second_moment, left_root, right_root)
     return pl.pallas_call(
         deliver,
         out_shape=(jax.ShapeDtypeStruct(updates.shape, BF16), stat, stat, stat),

time: 70.6 us -> 69.1 us (0.979)
  other arithmetic: 1.28 us -> 0 us
    reduce_sum x1 -> x0, other arithmetic: 1.28 us -> none  [per_device(): jnp.sum(jnp.where(block_owner[None, :] == indices[:, None], indices[None,...]
where the time goes in v4:
time: 69.1 us; the launch traced here: 68.9 us
  Pallas kernels  68.3 us (99%)
    pallas_call x1, Pallas kernels, per_device(): pl.pallas_call(kernel, out_shape=(jax.ShapeDtypeStruct((blocks, rows, wid...  66.5 us
    pallas_call x1, Pallas kernels, per_device(): pl.pallas_call(deliver, out_shape=(jax.ShapeDtypeStruct(updates.shape, BF...  1.74 us

profile of v4, /device:TPU:1, one launch (start us, length us, event | category | flops | bytes accessed | tf_op | source)
XLA Modules:
  0.0 68.9 jit_solution(7468681061699227079)
XLA Ops:
  0.6 66.5 %shard_map.111 = (bf16[16,16,512]{2,1,0:T(8,128)(2,1)}, f32[1,16,512]{2,1,0:T(8,128)}, f32[1,16,512]{2,1,0:T(8,128)}, f32[1,16,512]{2,1,0:T(8,128)}) custom-call(s32[16]{0:T(128)} %owner_ref.3, bf16[256,512]{1,0:T(8,128)(2,1)} %acts_hbm.1, bf16[256,2048]{1,0:T(8,128)(2,1)} %logit_ref.1, f32[1,16,512]{2,1,0:T(8,128)} %left_hbm.1, f32[1,16,512]{2,1,0:T(8,128)} %right_hbm.1, ...), custom_call_target="tpu_custom_call" | custom-call | tf_op jit(solution)/shard_map/pallas_call | solution.py:464
  67.2 1.7 %shard_map.112 = (bf16[16,16,512]{2,1,0:T(8,128)(2,1)}, f32[1,16,512]{2,1,0:T(8,128)}, f32[1,16,512]{2,1,0:T(8,128)}, f32[1,16,512]{2,1,0:T(8,128)}) custom-call(s32[16]{0:T(128)} %owner_ref.3, bf16[16,16,512]{2,1,0:T(8,128)(2,1)} %get-tuple-element.8.updates, f32[1,16,512]{2,1,0:T(8,128)} %get-tuple-element.9.left, f32[1,16,512]{2,1,0:T(8,128)} %get-tuple-element.10.right, ...), custom_call_target="tpu_custom_call" | custom-call | tf_op jit(solution)/shard_map/pallas_call | solution.py:505

commit v5 on v4

--- a/solution.py
+++ b/solution.py
@@ -187,7 +187,6 @@
     g_begin, g_middle, g_late, g_finish = gather(
         1, lambda q, core, column: grad.at[core, q, :, column], lambda q, core: grad.at[core, q]
     )
-    r_begin()
 
     def lroot_copy(k, column, device):
         return remote(
@@ -196,12 +195,6 @@
 
     def lroot_band(core):
         return remote(lroots.at[core], lroots.at[core], lroot_send.at[3], lroot_recv.at[1, 0], sibling)
-
-    lroot_load.wait()
-    for k, column in enumerate((x_far, x_next, x_prev)):
-        copy = lroot_copy(k, x, in_group(yl, c, column))
-        copy.start()
-        pending.append(copy)
 
     unit = band // NL
 
@@ -228,6 +221,13 @@
     acts_load.wait()
     acts_own = acts_ref[:, pl.ds(pl.multiple_of(c * half, half), half)]
     lax.fori_loop(0, blocks, own_block, 0, unroll=4)
+    r_begin()
+    lroot_load.wait()
+    for k, column in enumerate((x_far, x_next, x_prev)):
+        copy = lroot_copy(k, x, in_group(yl, c, column))
+        copy.start()
+        pending.append(copy)
+
     for copy in exchange:
         copy.wait_recv()
     pending.extend(exchange)
@@ -278,16 +278,7 @@
     r_middle()
     for step in range(1, 4):
         if step == 2:
-            for column in (x_next, x_prev, x_far):
-                lroot_copy(0, column, sibling).wait_recv()
-            copy = lroot_band(c)
-            copy.start()
-            pending.append(copy)
-            r_late(0)
-            r_late(1)
-        if step == 3:
-            r_late(2)
-            r_late(3)
+            pass
         for k in range(PIECES):
             for way in range(2):
                 piece = PIECE_ORDER[way][k]
@@ -313,6 +304,13 @@
 
     for k in range(1, 8):
         pending.append(axis_copy((me2 + k) % 8))
+    for k in range(NL):
+        r_late(k)
+    for column in (x_next, x_prev, x_far):
+        lroot_copy(0, column, sibling).wait_recv()
+    copy = lroot_band(c)
+    copy.start()
+    pending.append(copy)
     r_finish()
     lroot_band(1 - c).wait_recv()
     value = rroot[...].reshape(rroot_hi.shape)

time: 69.1 us -> 68.6 us (level)
  no operation moved by 1% of the time
where the time goes in v5:
time: 68.6 us; the launch traced here: 68.5 us
  Pallas kernels  67.8 us (99%)
    pallas_call x1, Pallas kernels, per_device(): pl.pallas_call(kernel, out_shape=(jax.ShapeDtypeStruct((blocks, rows, wid...  66.1 us
    pallas_call x1, Pallas kernels, per_device(): pl.pallas_call(deliver, out_shape=(jax.ShapeDtypeStruct(updates.shape, BF...  1.74 us

profile of v5, /device:TPU:1, one launch (start us, length us, event | category | flops | bytes accessed | tf_op | source)
XLA Modules:
  0.0 68.5 jit_solution(6998385088330415855)
XLA Ops:
  0.6 66.1 %shard_map.111 = (bf16[16,16,512]{2,1,0:T(8,128)(2,1)}, f32[1,16,512]{2,1,0:T(8,128)}, f32[1,16,512]{2,1,0:T(8,128)}, f32[1,16,512]{2,1,0:T(8,128)}) custom-call(s32[16]{0:T(128)} %owner_ref.3, bf16[256,512]{1,0:T(8,128)(2,1)} %acts_hbm.1, bf16[256,2048]{1,0:T(8,128)(2,1)} %logit_ref.1, f32[1,16,512]{2,1,0:T(8,128)} %left_hbm.1, f32[1,16,512]{2,1,0:T(8,128)} %right_hbm.1, ...), custom_call_target="tpu_custom_call" | custom-call | tf_op jit(solution)/shard_map/pallas_call | solution.py:462
  66.7 1.7 %shard_map.112 = (bf16[16,16,512]{2,1,0:T(8,128)(2,1)}, f32[1,16,512]{2,1,0:T(8,128)}, f32[1,16,512]{2,1,0:T(8,128)}, f32[1,16,512]{2,1,0:T(8,128)}) custom-call(s32[16]{0:T(128)} %owner_ref.3, bf16[16,16,512]{2,1,0:T(8,128)(2,1)} %get-tuple-element.8.updates, f32[1,16,512]{2,1,0:T(8,128)} %get-tuple-element.9.left, f32[1,16,512]{2,1,0:T(8,128)} %get-tuple-element.10.right, ...), custom_call_target="tpu_custom_call" | custom-call | tf_op jit(solution)/shard_map/pallas_call | solution.py:503

commit v6 on v5

--- a/solution.py
+++ b/solution.py
@@ -372,13 +372,13 @@
     precond[...] = precond_half(c).reshape(precond.shape)
     g_finish()
     chip_precond = precond[...].reshape(chip_rows, 2 * half) + precond_half(1 - c)
-    precond[...] = chip_precond.reshape(precond.shape)
 
     norms[yl] = jnp.broadcast_to(sum_all(chip_precond * chip_precond), (1, lanes))
     for k in (3, 2, 1):
         yl_to = (yl, yl + 1 - 2 * (yl % 2), (yl + 2) % NL, NL - 1 - yl)[k]
         remote(norms.at[yl], norms.at[yl], norm_send, norm_recv, in_group(yl_to, c, x)).start()
 
+    precond[...] = chip_precond.reshape(precond.shape)
     own = jnp.concatenate([grad[0, yl, c, x], grad[1, yl, c, x]], axis=1)
     moment_out[0] = 0.99 * moments[c] + 0.01 * own * own
 

time: 68.6 us -> 68.6 us (level)
  no operation moved by 1% of the time
where the time goes in v6:
time: 68.6 us; the launch traced here: 68.5 us
  Pallas kernels  67.8 us (99%)
    pallas_call x1, Pallas kernels, per_device(): pl.pallas_call(kernel, out_shape=(jax.ShapeDtypeStruct((blocks, rows, wid...  66.1 us
    pallas_call x1, Pallas kernels, per_device(): pl.pallas_call(deliver, out_shape=(jax.ShapeDtypeStruct(updates.shape, BF...  1.74 us

profile of v6, /device:TPU:1, one launch (start us, length us, event | category | flops | bytes accessed | tf_op | source)
XLA Modules:
  0.0 68.5 jit_solution(9784267881948913303)
XLA Ops:
  0.6 66.1 %shard_map.111 = (bf16[16,16,512]{2,1,0:T(8,128)(2,1)}, f32[1,16,512]{2,1,0:T(8,128)}, f32[1,16,512]{2,1,0:T(8,128)}, f32[1,16,512]{2,1,0:T(8,128)}) custom-call(s32[16]{0:T(128)} %owner_ref.3, bf16[256,512]{1,0:T(8,128)(2,1)} %acts_hbm.1, bf16[256,2048]{1,0:T(8,128)(2,1)} %logit_ref.1, f32[1,16,512]{2,1,0:T(8,128)} %left_hbm.1, f32[1,16,512]{2,1,0:T(8,128)} %right_hbm.1, ...), custom_call_target="tpu_custom_call" | custom-call | tf_op jit(solution)/shard_map/pallas_call | solution.py:462
  66.7 1.7 %shard_map.112 = (bf16[16,16,512]{2,1,0:T(8,128)(2,1)}, f32[1,16,512]{2,1,0:T(8,128)}, f32[1,16,512]{2,1,0:T(8,128)}, f32[1,16,512]{2,1,0:T(8,128)}) custom-call(s32[16]{0:T(128)} %owner_ref.3, bf16[16,16,512]{2,1,0:T(8,128)(2,1)} %get-tuple-element.8.updates, f32[1,16,512]{2,1,0:T(8,128)} %get-tuple-element.9.left, f32[1,16,512]{2,1,0:T(8,128)} %get-tuple-element.10.right, ...), custom_call_target="tpu_custom_call" | custom-call | tf_op jit(solution)/shard_map/pallas_call | solution.py:503
